TPU v7x, 32 devices: a whole 2x2x4 slice. The times are simulated.
32 devices in a mesh: tgt: 8 (over y, x, core), src: 4 (over z).
Axes of the slice: x: 2, y: 2, z: 4, core: 2. Of those that a mesh axis runs over, the one named last changes fastest.
Arguments:
- targets: float32 [8, 64, 4096], P('tgt'), may hold values from -8 to 8
- sources: float32 [8, 64, 4096], P('src', 'tgt'), may hold values from -8 to 8
- occupations: float32 [8], P('src'), may hold values from 0.2 to 2
Outputs:
- exchange_term: float32 [8, 64, 4096], P('tgt', 'src')
All inputs are finite; a program needn't handle non-finite values.
Results may differ from a plain program's by a relative error of at most 0.000076.
Values sent between devices are 32-bit elements; how exact they have to be, the bound alone decides.
A program may use at most 64 MiB of HBM per device.

v0:
```python
import functools
import math

import jax
import jax.numpy as jnp
import ml_dtypes
import numpy as np
from jax import lax
from jax.experimental import pallas as pl
from jax.experimental.pallas import tpu as pltpu
from jax.sharding import PartitionSpec as P

MESH = pl.DeviceIdType.MESH
LANES = 128


def split_table(table):
    high = table.astype(np.float32).astype(ml_dtypes.bfloat16)
    low = (table - high.astype(np.float64)).astype(np.float32).astype(ml_dtypes.bfloat16)
    return high, low


def basis(size):
    half = size // 2
    point = np.arange(size)
    freq = np.where(point <= half, point, point - half)
    angle = (freq[:, None] * point[None, :] % size) * (2.0 * math.pi / size)
    rows = np.where((point <= half)[:, None], np.cos(angle), np.sin(angle))
    norm = np.where((freq == 0) | (freq == half), 1.0, 2.0) / size
    return rows * np.sqrt(norm)[:, None], freq


def tables(size, count):
    rows, freq = basis(size)
    fold = LANES // size

    def left(matrix):
        high, low = split_table(matrix)
        return np.concatenate([high, high, low], axis=1)

    wide = np.zeros((count, fold, size, fold, count, size))
    for p in range(count):
        for y in range(fold):
            wide[p, y, :, y, p, :] = rows.T
    wide = wide.reshape(count * LANES, count * LANES)
    half = np.arange(size // 2 + 1).astype(np.float64)
    square = half[:, None, None] ** 2 + freq[None, :, None] ** 2 + freq[None, None, :] ** 2
    kern = (16.0 / (square + 0.25)).astype(np.float32)
    kern = np.concatenate([kern] * count, axis=-1)
    forward, inverse = split_table(wide), split_table(wide.T.copy())
    return left(rows), left(rows.T.copy()), *forward, *inverse, kern


def halves(value):
    high = value.astype(jnp.bfloat16)
    low = (value - high.astype(jnp.float32)).astype(jnp.bfloat16)
    return high, low


def dot(a, b):
    return jnp.dot(a, b, preferred_element_type=jnp.float32)


def from_left(table, value):
    high, low = halves(value)
    return dot(table, jnp.concatenate([high, low, high], axis=0))


def from_right(value, table_high, table_low):
    high, low = halves(value)
    return dot(high, table_high) + dot(low, table_high) + dot(high, table_low)


def body(shape, tgt, src, occ, left_f, left_i, right_fh, right_fl, right_ih, right_il, kern, out,
         whole, field, part, from_low, from_high, own_sem, send_sem, recv_sem, sum_send, low_recv, high_recv):
    nt, ns, count, size, chunks = shape
    width = size * size
    cut = width // chunks
    blocks = cut // LANES
    fold = LANES // size
    rows = part.shape[1]
    me, here = lax.axis_index("tgt"), lax.axis_index("src")
    chips = nt // 2
    chip, core = me // 2, me % 2
    mate = chip * 2 + (1 - core)

    def peer(step):
        return lax.rem(chip + step + chips, chips) * 2 + core

    barrier = pltpu.get_barrier_semaphore()
    for step in range(1, chips):
        pl.semaphore_signal(barrier, inc=1, device_id={"tgt": peer(step)}, device_id_type=MESH)
    pl.semaphore_signal(barrier, inc=1, device_id={"tgt": mate}, device_id_type=MESH)

    @pl.when(here > 0)
    def _():
        pl.semaphore_signal(barrier, inc=1, device_id={"src": here - 1}, device_id_type=MESH)

    @pl.when(here < ns - 1)
    def _():
        pl.semaphore_signal(barrier, inc=1, device_id={"src": here + 1}, device_id_type=MESH)

    own = pltpu.make_async_copy(src, whole.at[me], own_sem)
    own.start()
    inner = jnp.where(here > 0, 1, 0) + jnp.where(here < ns - 1, 1, 0)
    pl.semaphore_wait(barrier, chips + inner)

    def piece(c):
        return pl.ds(c * cut, cut)

    def send(c, slot, origin, target, source):
        return pltpu.make_async_remote_copy(
            src_ref=source.at[:, :, piece(c)],
            dst_ref=whole.at[origin, :, :, piece(c)],
            send_sem=send_sem.at[c, slot],
            recv_sem=recv_sem.at[c, origin],
            device_id={"tgt": target},
            device_id_type=MESH,
        )

    def arrived(c, origin):
        send(c, 0, origin, mate, src).wait_recv()

    sent = []
    for c in range(chunks):
        for step in range(1, chips):
            sent.append(send(c, step, me, peer(step), src))
            sent[-1].start()
        sent.append(send(c, 0, me, mate, src))
        sent[-1].start()
    own.wait()

    def source_block(p, cols):
        return jnp.concatenate([whole[t, p, :, cols] for t in range(nt)], axis=0)

    def columns(j):
        return pl.ds(pl.multiple_of(j * LANES, LANES), LANES)

    def forward_block(j, carry):
        cols = columns(j)
        target = tgt[0, :, cols]
        pair = jnp.concatenate([target * source_block(p, cols) for p in range(count)], axis=1)
        value = from_right(from_left(left_f[...], pair), right_fh[...], right_fl[...])
        for y in range(fold):
            at = pl.multiple_of((j * fold + y) * size, size)
            field[pl.ds(at, size), :] = value[:, y * count * size:(y + 1) * count * size]
        return carry

    def partner_arrived(c):
        arrived(c, mate)
        for step in range(1, chips):
            arrived(c, lax.rem(chip + step, chips) * 2 + 1 - core)

    for c in range(chunks + 1):
        if c < chunks:
            for step in range(1, chips):
                origin = peer(-step)
                arrived(c, origin)
                sent.append(send(c, chips - 1 + step, origin, mate, whole.at[origin]))
                sent[-1].start()
        if c > 0:
            partner_arrived(c - 1)
            lax.fori_loop((c - 1) * blocks, c * blocks, forward_block, 0)

    def middle(k, carry):
        first = k * 2
        value = jnp.concatenate(
            [field[pl.ds(first + i, size, stride=size), :] for i in range(2)], axis=1)
        scale = []
        for i in range(2):
            index = first + i
            scale.append(kern[jnp.where(index > size // 2, index - size // 2, index)])
        value = from_left(left_f[...], value) * jnp.concatenate(scale, axis=1)
        value = from_left(left_i[...], value)
        for i in range(2):
            lanes = count * size
            field[pl.ds(first + i, size, stride=size), :] = value[:, i * lanes:(i + 1) * lanes]
        return carry

    lax.fori_loop(0, size // 2, middle, 0)

    def inverse_block(j, carry):
        cols = columns(j)
        value = jnp.concatenate(
            [field[pl.ds(pl.multiple_of((j * fold + y) * size, size), size), :] for y in range(fold)], axis=1)
        value = from_left(left_i[...], from_right(value, right_ih[...], right_il[...]))
        total = None
        for p in range(count):
            term = (value[:, p * LANES:(p + 1) * LANES] * source_block(p, cols)) * occ[p]
            total = term if total is None else total + term
        total = -total
        for d in range(ns):
            part[d, :, cols] = total[d * rows:(d + 1) * rows, :]
        return carry

    order = []
    for d in range((ns + 1) // 2):
        order += [ns - 1 - d] + ([d] if d != ns - 1 - d else [])

    def pass_on(c, d, upward):
        buffer, sems = (from_low, low_recv) if upward else (from_high, high_recv)
        return pltpu.make_async_remote_copy(
            src_ref=part.at[d, :, piece(c)],
            dst_ref=buffer.at[d, :, piece(c)],
            send_sem=sum_send.at[c, d],
            recv_sem=sems.at[c, d],
            device_id={"src": here + 1 if upward else here - 1},
            device_id_type=MESH,
        )

    def start_ends(c):
        for d in order:
            if d > 0:
                @pl.when(here == 0)
                def _():
                    pass_on(c, d, True).start()
            if d < ns - 1:
                @pl.when(here == ns - 1)
                def _():
                    pass_on(c, d, False).start()

    def relay(c):
        for d in order:
            if d > 1:
                @pl.when((here > 0) & (here < d))
                def _():
                    pass_on(c, d, True).wait_recv()
                    part[d, :, piece(c)] += from_low[d, :, piece(c)]
                    pass_on(c, d, True).start()
            if d < ns - 2:
                @pl.when((here < ns - 1) & (here > d))
                def _():
                    pass_on(c, d, False).wait_recv()
                    part[d, :, piece(c)] += from_high[d, :, piece(c)]
                    pass_on(c, d, False).start()

    def finish(c):
        out[0, :, piece(c)] = part[here, :, piece(c)]

        @pl.when(here > 0)
        def _():
            pass_on(c, here, True).wait_recv()
            out[0, :, piece(c)] += from_low[here, :, piece(c)]

        @pl.when(here < ns - 1)
        def _():
            pass_on(c, here, False).wait_recv()
            out[0, :, piece(c)] += from_high[here, :, piece(c)]

    for c in range(chunks):
        lax.fori_loop(c * blocks, (c + 1) * blocks, inverse_block, 0)
        start_ends(c)
        if c > 0:
            relay(c - 1)
    relay(chunks - 1)
    for c in range(chunks):
        finish(c)

    for copy in sent:
        copy.wait_send()
    for c in range(chunks):
        for d in range(ns):
            @pl.when(here != d)
            def _():
                pass_on(c, d, True).wait_send()


def on_device(nt, ns, targets, sources, occupations):
    size, width = targets.shape[1], targets.shape[2]
    count, slab = sources.shape[0], sources.shape[1]
    rows = size // ns
    chunks = 4
    consts = [jnp.asarray(t) for t in tables(size, count)]
    vmem = pl.BlockSpec(memory_space=pltpu.VMEM)
    smem = pl.BlockSpec(memory_space=pltpu.SMEM)
    return pl.pallas_call(
        functools.partial(body, (nt, ns, count, size, chunks)),
        out_shape=jax.ShapeDtypeStruct((1, rows, width), jnp.float32),
        in_specs=[vmem, vmem, smem] + [vmem] * len(consts),
        out_specs=vmem,
        scratch_shapes=[
            pltpu.VMEM((nt, count, slab, width), jnp.float32),
            pltpu.VMEM((size * size, count * size), jnp.float32),
            pltpu.VMEM((ns, rows, width), jnp.float32),
            pltpu.VMEM((ns, rows, width), jnp.float32),
            pltpu.VMEM((ns, rows, width), jnp.float32),
            pltpu.SemaphoreType.DMA,
            pltpu.SemaphoreType.DMA((chunks, nt)),
            pltpu.SemaphoreType.DMA((chunks, nt)),
            pltpu.SemaphoreType.DMA((chunks, ns)),
            pltpu.SemaphoreType.DMA((chunks, ns)),
            pltpu.SemaphoreType.DMA((chunks, ns)),
        ],
        compiler_params=pltpu.CompilerParams(
            collective_id=0, has_side_effects=True, vmem_limit_bytes=48 * 1024 * 1024
        ),
    )(targets, sources, occupations, *consts)


def solution(mesh):
    return jax.shard_map(
        functools.partial(on_device, mesh.shape["tgt"], mesh.shape["src"]),
        mesh=mesh,
        in_specs=(P("tgt", None, None), P("src", "tgt", None), P("src")),
        out_specs=P("tgt", "src", None),
        check_vma=False,
    )
```

profile of v0, /device:TPU:0, one launch (start us, length us, event | category | flops | bytes accessed | tf_op | source)
XLA Modules:
  0.0 89.2 jit_solution(12768142767057527805)
XLA Ops:
  0.0 0.0 copy-start
  0.0 1.2 %copy-done = f32[33,64,128]{2,1,0:T(8,128)S(1)} copy-done((f32[33,64,128]{2,1,0:T(8,128)S(1)}, f32[33,64,128]{2,1,0:T(8,128)}, u32[]{:S(2)}) %copy-start) | copy-done | bytes 1081368
  1.2 0.0 copy-start.1
  1.2 1.2 %copy-done.1 = f32[1,64,4096]{2,1,0:T(8,128)S(1)} copy-done((f32[1,64,4096]{2,1,0:T(8,128)S(1)}, f32[1,64,4096]{2,1,0:T(8,128)}, u32[]{:S(2)}) %copy-start.1) | copy-done | bytes 1048600
  2.5 0.0 copy-start.2
  2.5 0.9 %copy-done.2 = f32[2,8,4096]{2,1,0:T(8,128)S(1)} copy-done((f32[2,8,4096]{2,1,0:T(8,128)S(1)}, f32[2,8,4096]{2,1,0:T(8,128)}, u32[]{:S(2)}) %copy-start.2) | copy-done | bytes 262168
  3.4 0.0 copy-start.3
  3.4 0.9 %copy-done.3 = bf16[256,256]{1,0:T(8,128)(2,1)S(1)} copy-done((bf16[256,256]{1,0:T(8,128)(2,1)S(1)}, bf16[256,256]{1,0:T(8,128)(2,1)}, u32[]{:S(2)}) %copy-start.3) | copy-done | bytes 131096
  4.3 0.0 copy-start.4
  4.3 0.9 %copy-done.4 = bf16[256,256]{1,0:T(8,128)(2,1)S(1)} copy-done((bf16[256,256]{1,0:T(8,128)(2,1)S(1)}, bf16[256,256]{1,0:T(8,128)(2,1)}, u32[]{:S(2)}) %copy-start.4) | copy-done | bytes 131096
  5.2 0.0 copy-start.5
  5.2 0.9 %copy-done.5 = bf16[256,256]{1,0:T(8,128)(2,1)S(1)} copy-done((bf16[256,256]{1,0:T(8,128)(2,1)S(1)}, bf16[256,256]{1,0:T(8,128)(2,1)}, u32[]{:S(2)}) %copy-start.5) | copy-done | bytes 131096
  6.1 0.0 copy-start.6
  6.1 0.9 %copy-done.6 = bf16[256,256]{1,0:T(8,128)(2,1)S(1)} copy-done((bf16[256,256]{1,0:T(8,128)(2,1)S(1)}, bf16[256,256]{1,0:T(8,128)(2,1)}, u32[]{:S(2)}) %copy-start.6) | copy-done | bytes 131096
  7.0 0.0 copy-start.7
  7.0 0.8 copy-done.7
  7.8 0.0 copy-start.8
  7.8 0.8 copy-done.8
  8.5 0.0 copy-start.9
  8.6 0.7 copy-done.9
  9.2 79.3 %shard_map.100 = f32[1,16,4096]{2,1,0:T(8,128)S(1)} custom-call(f32[1,64,4096]{2,1,0:T(8,128)S(1)} %copy-done.1, f32[2,8,4096]{2,1,0:T(8,128)S(1)} %copy-done.2, f32[2]{0:T(128)S(1)} %copy-done.9, bf16[64,192]{1,0:T(8,128)(2,1)S(1)} %copy-done.8, bf16[64,192]{1,0:T(8,128)(2,1)S(1)} %copy-done.7, bf16[256,256]{1,0:T(8,128)(2,1)S(1)} %copy-done.6, ...), custom_call_target="tpu_custom_call" | custom-call | tf_op jit(solution)/shard_map/pallas_call | solution.py:276
  88.5 0.7 copy.12
Async XLA Ops:
  0.0 1.2 %copy-start = (f32[33,64,128]{2,1,0:T(8,128)S(1)}, f32[33,64,128]{2,1,0:T(8,128)}, u32[]{:S(2)}) copy-start(f32[33,64,128]{2,1,0:T(8,128)} %constant.20.clone.kern) | copy-start | bytes 3244036
  1.2 1.2 %copy-start.1 = (f32[1,64,4096]{2,1,0:T(8,128)S(1)}, f32[1,64,4096]{2,1,0:T(8,128)}, u32[]{:S(2)}) copy-start(f32[1,64,4096]{2,1,0:T(8,128)} %tgt.1) | copy-start | bytes 3145732
  2.5 0.9 %copy-start.2 = (f32[2,8,4096]{2,1,0:T(8,128)S(1)}, f32[2,8,4096]{2,1,0:T(8,128)}, u32[]{:S(2)}) copy-start(f32[2,8,4096]{2,1,0:T(8,128)} %src.1) | copy-start | bytes 786436
  3.4 0.9 %copy-start.3 = (bf16[256,256]{1,0:T(8,128)(2,1)S(1)}, bf16[256,256]{1,0:T(8,128)(2,1)}, u32[]{:S(2)}) copy-start(bf16[256,256]{1,0:T(8,128)(2,1)} %constant.19.clone.right_il) | copy-start | bytes 393220
  4.3 0.9 %copy-start.4 = (bf16[256,256]{1,0:T(8,128)(2,1)S(1)}, bf16[256,256]{1,0:T(8,128)(2,1)}, u32[]{:S(2)}) copy-start(bf16[256,256]{1,0:T(8,128)(2,1)} %constant.18.clone.right_ih) | copy-start | bytes 393220
  5.2 0.9 %copy-start.5 = (bf16[256,256]{1,0:T(8,128)(2,1)S(1)}, bf16[256,256]{1,0:T(8,128)(2,1)}, u32[]{:S(2)}) copy-start(bf16[256,256]{1,0:T(8,128)(2,1)} %constant.17.clone.right_fl) | copy-start | bytes 393220
  6.1 0.9 %copy-start.6 = (bf16[256,256]{1,0:T(8,128)(2,1)S(1)}, bf16[256,256]{1,0:T(8,128)(2,1)}, u32[]{:S(2)}) copy-start(bf16[256,256]{1,0:T(8,128)(2,1)} %constant.16.clone.right_fh) | copy-start | bytes 393220
  7.0 0.8 copy-start.7
  7.8 0.8 copy-start.8
  8.5 0.7 copy-start.9
where the time goes:
time: 89.7 us; the launch traced here: 89.2 us
  Pallas kernels  79.3 us (88%)
  local copies, waits for them, and re-layouts  9.9 us (11%)
    pallas_call x1, Pallas kernels, on_device(): pl.pallas_call(functools.partial(body, (nt, ns, count, size, chunks)), ou...  79.3 us
    unnamed x21, local copies, waits for them, and re-layouts  9.9 us

commit v1 on v0

v1 whole, which is shorter than its diff:
```python
import functools
import math

import jax
import jax.numpy as jnp
import ml_dtypes
import numpy as np
from jax import lax
from jax.experimental import pallas as pl
from jax.experimental.pallas import tpu as pltpu
from jax.sharding import PartitionSpec as P

MESH = pl.DeviceIdType.MESH
LANES = 128
CHUNKS = 4
BATCH = 8
GROUP = 16


def split_table(table):
    high = table.astype(np.float32).astype(ml_dtypes.bfloat16)
    low = (table - high.astype(np.float64)).astype(np.float32).astype(ml_dtypes.bfloat16)
    return high, low


def basis(size):
    half = size // 2
    point = np.arange(size)
    freq = np.where(point <= half, point, point - half)
    angle = (freq[:, None] * point[None, :] % size) * (2.0 * math.pi / size)
    rows = np.where((point <= half)[:, None], np.cos(angle), np.sin(angle))
    norm = np.where((freq == 0) | (freq == half), 1.0, 2.0) / size
    return rows * np.sqrt(norm)[:, None], freq


def tables(size, count):
    rows, freq = basis(size)
    fold = LANES // size

    def left(matrix):
        high, low = split_table(matrix)
        return np.concatenate([high, high, low], axis=1)

    wide = np.zeros((count, fold, size, fold, count, size))
    for p in range(count):
        for y in range(fold):
            wide[p, y, :, y, p, :] = rows.T
    wide = wide.reshape(count * LANES, count * LANES)
    half = np.arange(size // 2 + 1).astype(np.float64)
    square = half[:, None, None] ** 2 + freq[None, :, None] ** 2 + freq[None, None, :] ** 2
    kern = (16.0 / (square + 0.25)).astype(np.float32)
    kern = np.concatenate([kern] * count, axis=-1)
    forward, inverse = split_table(wide), split_table(wide.T.copy())
    lefts = np.stack([left(rows), left(rows.T.copy())])
    return lefts, np.stack([*forward, *inverse]), kern


def halves(value):
    high = value.astype(jnp.bfloat16)
    low = (value - high.astype(jnp.float32)).astype(jnp.bfloat16)
    return high, low


def dot(a, b):
    return jnp.dot(a, b, preferred_element_type=jnp.float32)


def from_left(table, value):
    high, low = halves(value)
    return dot(table, jnp.concatenate([high, low, high], axis=0))


def from_right(value, table_high, table_low):
    high, low = halves(value)
    return dot(high, table_high) + dot(low, table_high) + dot(high, table_low)


def body(shape, tgt_any, src_any, occ, left_any, right_any, kern_any, out,
         tgt, left, right, kern, load_sem, whole, field, part, inbox, relay, own_sem, send_sem, recv_sem, sum_send, sum_recv, relay_recv):
    nt, ns, count, size, chunks = shape
    width = size * size
    cut = width // chunks
    batch = math.gcd(BATCH, cut // LANES)
    loops = cut // LANES // batch
    group = math.gcd(GROUP, size)
    fold = LANES // size
    rows = part.shape[1]
    me, here = lax.axis_index("tgt"), lax.axis_index("src")
    chips = nt // 2
    chip, core = me // 2, me % 2
    mate = chip * 2 + (1 - core)

    def peer(step):
        return lax.rem(chip + step + chips, chips) * 2 + core

    barrier = pltpu.get_barrier_semaphore()
    for step in range(1, chips):
        pl.semaphore_signal(barrier, inc=1, device_id={"tgt": peer(step)}, device_id_type=MESH)
    pl.semaphore_signal(barrier, inc=1, device_id={"tgt": mate}, device_id_type=MESH)

    for step in range(1, ns):
        pl.semaphore_signal(barrier, inc=1, device_id={"src": lax.rem(here + step, ns)}, device_id_type=MESH)

    own = pltpu.make_async_copy(src_any, whole.at[me], own_sem)
    own.start()
    src = whole.at[me]
    loads = [
        pltpu.make_async_copy(here_ref, there_ref, load_sem.at[i])
        for i, (here_ref, there_ref) in enumerate(
            [(left_any, left), (right_any, right), (tgt_any, tgt), (kern_any, kern)])
    ]
    for load in loads:
        load.start()
    pl.semaphore_wait(barrier, chips + ns - 1)

    def piece(c):
        return pl.ds(c * cut, cut)

    def send(c, slot, origin, target, source):
        return pltpu.make_async_remote_copy(
            src_ref=source.at[:, :, piece(c)],
            dst_ref=whole.at[origin, :, :, piece(c)],
            send_sem=send_sem.at[c, slot],
            recv_sem=recv_sem.at[c, origin],
            device_id={"tgt": target},
            device_id_type=MESH,
        )

    def arrived(c, origin):
        send(c, 0, origin, mate, src).wait_recv()

    own.wait()
    sent = []
    for c in range(chunks):
        for step in range(1, chips):
            sent.append(send(c, step, me, peer(step), src))
            sent[-1].start()
        sent.append(send(c, 0, me, mate, src))
        sent[-1].start()
    for load in loads[:3]:
        load.wait()

    def source_block(p, cols):
        return jnp.concatenate([whole[t, p, :, cols] for t in range(nt)], axis=0)

    def columns(j):
        return pl.ds(pl.multiple_of(j * LANES, LANES), LANES)

    def stacked(value):
        wide = count * LANES
        return jnp.concatenate([value[:, b * wide:(b + 1) * wide] for b in range(batch)], axis=0)

    def unstacked(value):
        return jnp.concatenate([value[b * size:(b + 1) * size] for b in range(batch)], axis=1)

    def forward_blocks(i, carry):
        pairs = []
        for b in range(batch):
            cols = columns(i * batch + b)
            target = tgt[0, :, cols]
            pairs += [target * source_block(p, cols) for p in range(count)]
        value = stacked(from_left(left[0], jnp.concatenate(pairs, axis=1)))
        value = from_right(value, right[0], right[1])
        for b in range(batch):
            for y in range(fold):
                at = pl.multiple_of(((i * batch + b) * fold + y) * size, size)
                field[pl.ds(at, size), :] = value[
                    b * size:(b + 1) * size, y * count * size:(y + 1) * count * size]
        return carry

    def partner_arrived(c):
        arrived(c, mate)
        for step in range(1, chips):
            arrived(c, lax.rem(chip + step, chips) * 2 + 1 - core)

    for c in range(chunks + 1):
        if c < chunks:
            for step in range(1, chips):
                origin = peer(-step)
                arrived(c, origin)
                sent.append(send(c, chips - 1 + step, origin, mate, whole.at[origin]))
                sent[-1].start()
        if c > 0:
            partner_arrived(c - 1)
            lax.fori_loop((c - 1) * loops, c * loops, forward_blocks, 0)

    def middle(k, carry):
        lanes = count * size
        first = k * group
        value = jnp.concatenate(
            [field[pl.ds(first + i, size, stride=size), :] for i in range(group)], axis=1)
        scale = []
        for i in range(group):
            index = first + i
            scale.append(kern[jnp.where(index > size // 2, index - size // 2, index)])
        value = from_left(left[0], value) * jnp.concatenate(scale, axis=1)
        value = from_left(left[1], value)
        for i in range(group):
            field[pl.ds(first + i, size, stride=size), :] = value[:, i * lanes:(i + 1) * lanes]
        return carry

    loads[3].wait()
    lax.fori_loop(0, size // group, middle, 0)

    def inverse_blocks(i, carry):
        value = jnp.concatenate([
            jnp.concatenate([
                field[pl.ds(pl.multiple_of(((i * batch + b) * fold + y) * size, size), size), :]
                for y in range(fold)], axis=1)
            for b in range(batch)], axis=0)
        value = from_left(left[1], unstacked(from_right(value, right[2], right[3])))
        for b in range(batch):
            cols = columns(i * batch + b)
            total = None
            for p in range(count):
                at = (b * count + p) * LANES
                term = value[:, at:at + LANES] * source_block(p, cols) * occ[p]
                total = term if total is None else total + term
            total = -total
            for d in range(ns):
                part[d, :, cols] = total[d * rows:(d + 1) * rows, :]
        return carry

    relayed = ns >= 4
    last = ns - 1

    def term(c, d):
        return pltpu.make_async_remote_copy(
            src_ref=part.at[d, :, piece(c)],
            dst_ref=inbox.at[here, :, piece(c)],
            send_sem=sum_send.at[c, d],
            recv_sem=sum_recv.at[c, here],
            device_id={"src": d},
            device_id_type=MESH,
        )

    def term_arrived(c, origin):
        pltpu.make_async_remote_copy(
            src_ref=part.at[0, :, piece(c)],
            dst_ref=inbox.at[origin, :, piece(c)],
            send_sem=sum_send.at[c, 0],
            recv_sem=sum_recv.at[c, origin],
            device_id={"src": origin},
            device_id_type=MESH,
        ).wait_recv()

    def far(c, upward):
        return pltpu.make_async_remote_copy(
            src_ref=part.at[last if upward else 0, :, piece(c)],
            dst_ref=relay.at[:, piece(c)],
            send_sem=sum_send.at[c, last if upward else 0],
            recv_sem=relay_recv.at[c],
            device_id={"src": 1 if upward else last - 1},
            device_id_type=MESH,
        )

    def start_far(c):
        if relayed:
            for end in (0, last):
                @pl.when(here == end)
                def _():
                    far(c, end == 0).start()

    def start_near(c, s):
        order = sorted((d for d in range(ns) if d != s), key=lambda d: -abs(d - s))
        for d in order:
            if not (relayed and (d == last and s in (0, 1) or d == 0 and s in (last, last - 1))):
                term(c, d).start()

    def start_relay(c):
        if relayed:
            for s, d in ((1, last), (last - 1, 0)):
                @pl.when(here == s)
                def _():
                    far(c, s == 1).wait_recv()
                    part[d, :, piece(c)] += relay[:, piece(c)]
                    term(c, d).start()

    def middles(c):
        for s in range(1, last):
            @pl.when(here == s)
            def _():
                start_near(c, s)

    def ends(c):
        for s in (0, last):
            @pl.when(here == s)
            def _():
                start_near(c, s)

    def finish(c):
        out[0, :, piece(c)] = part[here, :, piece(c)]
        for o in range(ns):
            there = here != o
            if relayed and o in (0, last):
                there = there & (here != last - o)

            @pl.when(there)
            def _():
                term_arrived(c, o)
                out[0, :, piece(c)] += inbox[o, :, piece(c)]

    for c in range(chunks):
        lax.fori_loop(c * loops, (c + 1) * loops, inverse_blocks, 0)
        start_far(c)
        middles(c)
        if c > 0:
            ends(c - 1)
            start_relay(c - 1)
    ends(chunks - 1)
    start_relay(chunks - 1)
    for c in range(chunks):
        finish(c)

    for copy in sent:
        copy.wait_send()
    for c in range(chunks):
        for d in range(ns):
            @pl.when(here != d)
            def _():
                term(c, d).wait_send()


def on_device(nt, ns, targets, sources, occupations):
    size, width = targets.shape[1], targets.shape[2]
    count, slab = sources.shape[0], sources.shape[1]
    rows = size // ns
    chunks = CHUNKS
    consts = [jnp.asarray(t) for t in tables(size, count)]
    vmem = pl.BlockSpec(memory_space=pltpu.VMEM)
    hbm = pl.BlockSpec(memory_space=pl.ANY)
    smem = pl.BlockSpec(memory_space=pltpu.SMEM)
    return pl.pallas_call(
        functools.partial(body, (nt, ns, count, size, chunks)),
        out_shape=jax.ShapeDtypeStruct((1, rows, width), jnp.float32),
        in_specs=[hbm, hbm, smem] + [hbm] * len(consts),
        out_specs=vmem,
        scratch_shapes=[
            pltpu.VMEM(targets.shape, jnp.float32),
            *(pltpu.VMEM(t.shape, t.dtype) for t in consts),
            pltpu.SemaphoreType.DMA((1 + len(consts),)),
            pltpu.VMEM((nt, count, slab, width), jnp.float32),
            pltpu.VMEM((size * size, count * size), jnp.float32),
            pltpu.VMEM((ns, rows, width), jnp.float32),
            pltpu.VMEM((ns, rows, width), jnp.float32),
            pltpu.VMEM((rows, width), jnp.float32),
            pltpu.SemaphoreType.DMA,
            pltpu.SemaphoreType.DMA((chunks, nt)),
            pltpu.SemaphoreType.DMA((chunks, nt)),
            pltpu.SemaphoreType.DMA((chunks, ns)),
            pltpu.SemaphoreType.DMA((chunks, ns)),
            pltpu.SemaphoreType.DMA((chunks,)),
        ],
        compiler_params=pltpu.CompilerParams(
            collective_id=0, has_side_effects=True, vmem_limit_bytes=63 * 1024 * 1024
        ),
    )(targets, sources, occupations, *consts)


def solution(mesh):
    return jax.shard_map(
        functools.partial(on_device, mesh.shape["tgt"], mesh.shape["src"]),
        mesh=mesh,
        in_specs=(P("tgt", None, None), P("src", "tgt", None), P("src")),
        out_specs=P("tgt", "src", None),
        check_vma=False,
    )
```

time: 89.7 us -> 48.5 us (0.54)
  Pallas kernels: 79.3 us -> 46.7 us
  local copies, waits for them, and re-layouts: 9.9 us -> 1.67 us
    pallas_call x1, Pallas kernels: 79.3 us -> 46.7 us  [on_device(): pl.pallas_call(functools.partial(body, (nt, ns, count, size, chunks)), ou...]
    unnamed x21 -> x1, local copies, waits for them, and re-layouts: 9.9 us -> 1.67 us
where the time goes in v1:
time: 48.5 us; the launch traced here: 48.4 us
  Pallas kernels  46.7 us (96%)
  local copies, waits for them, and re-layouts  1.67 us (3%)
    pallas_call x1, Pallas kernels, on_device(): pl.pallas_call(functools.partial(body, (nt, ns, count, size, chunks)), ou...  46.7 us
    unnamed x1, local copies, waits for them, and re-layouts  1.67 us

profile of v1, /device:TPU:0, one launch (start us, length us, event | category | flops | bytes accessed | tf_op | source)
XLA Modules:
  0.0 48.4 jit_solution(12028229035650917178)
XLA Ops:
  0.0 46.7 %shard_map.64 = f32[1,16,4096]{2,1,0:T(8,128)} custom-call(f32[1,64,4096]{2,1,0:T(8,128)} %tgt_any.1, f32[2,8,4096]{2,1,0:T(8,128)} %src_any.1, f32[2]{0:T(128)} %occ.1, bf16[2,64,192]{2,1,0:T(8,128)(2,1)} %constant.6.clone.left_any, bf16[4,256,256]{2,1,0:T(8,128)(2,1)} %constant.7.clone.right_any, f32[33,64,128]{2,1,0:T(8,128)} %constant.8.clone.kern_any), custom_call_target="tpu_custom_call" | custom-call | tf_op jit(solution)/shard_map/pallas_call | solution.py:333
  46.7 1.7 %copy.8 = f32[1,16,4096]{2,1,0:T(8,128)} copy(f32[1,16,4096]{2,1,0:T(8,128)} %shard_map.64) | data formatting | bytes 524288

commit v2 on v1

--- a/solution.py
+++ b/solution.py
@@ -116,27 +116,81 @@
     def piece(c):
         return pl.ds(c * cut, cut)
 
-    def send(c, slot, origin, target, source):
+    across, beyond, corner = chip + 1 - 2 * (chip % 2), lax.rem(chip + 2, 4), 3 - chip
+    folded = chips == 4
+    near, rest = (0, (count + 1) // 2), ((count + 1) // 2, count - (count + 1) // 2)
+    all_of = (0, count)
+
+    def copy_of(c, out_slot, in_slot, origin, target, source, span):
         return pltpu.make_async_remote_copy(
-            src_ref=source.at[:, :, piece(c)],
-            dst_ref=whole.at[origin, :, :, piece(c)],
-            send_sem=send_sem.at[c, slot],
-            recv_sem=recv_sem.at[c, origin],
+            src_ref=source.at[pl.ds(*span), :, piece(c)],
+            dst_ref=whole.at[origin, pl.ds(*span), :, piece(c)],
+            send_sem=send_sem.at[c, out_slot],
+            recv_sem=recv_sem.at[c, in_slot],
             device_id={"tgt": target},
             device_id_type=MESH,
         )
 
-    def arrived(c, origin):
-        send(c, 0, origin, mate, src).wait_recv()
+    sent = []
+
+    def send(c, out_slot, in_slot, origin, target, source, span=all_of):
+        sent.append(copy_of(c, out_slot, in_slot, origin, target, source, span))
+        sent[-1].start()
+
+    def arrived(c, in_slot, origin, span=all_of):
+        copy_of(c, 0, in_slot, origin, mate, whole.at[origin], span).wait_recv()
+
+    def at(place):
+        return place * 2 + core
+
+    def beside(place):
+        return place * 2 + 1 - core
+
+    def first_hop(c):
+        if folded:
+            send(c, 0, 0, me, at(across), src)
+            send(c, 1, 1, me, at(beyond), src)
+            send(c, 2, 4, me, mate, src)
+        else:
+            for step in range(1, chips):
+                send(c, step, me, me, peer(step), src)
+            send(c, 0, me, me, mate, src)
+
+    def second_hop(c):
+        if folded:
+            arrived(c, 0, at(across))
+            send(c, 3, 2, at(across), at(beyond), whole.at[at(across)], near)
+            arrived(c, 1, at(beyond))
+            send(c, 4, 3, at(beyond), at(across), whole.at[at(beyond)], rest)
+            send(c, 5, 5, at(across), mate, whole.at[at(across)])
+            send(c, 6, 6, at(beyond), mate, whole.at[at(beyond)])
+        else:
+            for step in range(1, chips):
+                origin = peer(-step)
+                arrived(c, origin, origin)
+                send(c, chips - 1 + step, origin, origin, mate, whole.at[origin])
+
+    def third_hop(c):
+        if folded:
+            arrived(c, 2, at(corner), near)
+            arrived(c, 3, at(corner), rest)
+            send(c, 7, 7, at(corner), mate, whole.at[at(corner)])
+
+    def complete(c):
+        if folded:
+            arrived(c, 4, mate)
+            arrived(c, 5, beside(across))
+            arrived(c, 6, beside(beyond))
+            arrived(c, 7, beside(corner))
+        else:
+            arrived(c, mate, mate)
+            for step in range(1, chips):
+                origin = beside(lax.rem(chip + step, chips))
+                arrived(c, origin, origin)
 
     own.wait()
-    sent = []
     for c in range(chunks):
-        for step in range(1, chips):
-            sent.append(send(c, step, me, peer(step), src))
-            sent[-1].start()
-        sent.append(send(c, 0, me, mate, src))
-        sent[-1].start()
+        first_hop(c)
     for load in loads[:3]:
         load.wait()
 
@@ -163,26 +217,19 @@
         value = from_right(value, right[0], right[1])
         for b in range(batch):
             for y in range(fold):
-                at = pl.multiple_of(((i * batch + b) * fold + y) * size, size)
-                field[pl.ds(at, size), :] = value[
+                row = pl.multiple_of(((i * batch + b) * fold + y) * size, size)
+                field[pl.ds(row, size), :] = value[
                     b * size:(b + 1) * size, y * count * size:(y + 1) * count * size]
         return carry
 
-    def partner_arrived(c):
-        arrived(c, mate)
-        for step in range(1, chips):
-            arrived(c, lax.rem(chip + step, chips) * 2 + 1 - core)
-
-    for c in range(chunks + 1):
-        if c < chunks:
-            for step in range(1, chips):
-                origin = peer(-step)
-                arrived(c, origin)
-                sent.append(send(c, chips - 1 + step, origin, mate, whole.at[origin]))
-                sent[-1].start()
-        if c > 0:
-            partner_arrived(c - 1)
-            lax.fori_loop((c - 1) * loops, c * loops, forward_blocks, 0)
+    for step in range(chunks + 2):
+        if step < chunks:
+            second_hop(step)
+        if step >= 2:
+            complete(step - 2)
+            lax.fori_loop((step - 2) * loops, (step - 1) * loops, forward_blocks, 0)
+        if 1 <= step <= chunks:
+            third_hop(step - 1)
 
     def middle(k, carry):
         lanes = count * size
@@ -213,8 +260,8 @@
             cols = columns(i * batch + b)
             total = None
             for p in range(count):
-                at = (b * count + p) * LANES
-                term = value[:, at:at + LANES] * source_block(p, cols) * occ[p]
+                lane = (b * count + p) * LANES
+                term = value[:, lane:lane + LANES] * source_block(p, cols) * occ[p]
                 total = term if total is None else total + term
             total = -total
             for d in range(ns):

time: 48.5 us -> 46.3 us (0.955)
  Pallas kernels: 46.7 us -> 44.4 us
    pallas_call x1, Pallas kernels: 46.7 us -> 44.4 us  [on_device(): pl.pallas_call(functools.partial(body, (nt, ns, count, size, chunks)), ou...]
where the time goes in v2:
time: 46.3 us; the launch traced here: 46.1 us
  Pallas kernels  44.4 us (96%)
  local copies, waits for them, and re-layouts  1.67 us (4%)
    pallas_call x1, Pallas kernels, on_device(): pl.pallas_call(functools.partial(body, (nt, ns, count, size, chunks)), ou...  44.4 us
    unnamed x1, local copies, waits for them, and re-layouts  1.67 us

profile of v2, /device:TPU:0, one launch (start us, length us, event | category | flops | bytes accessed | tf_op | source)
XLA Modules:
  0.0 46.1 jit_solution(6097901275286785998)
XLA Ops:
  0.0 44.4 %shard_map.64 = f32[1,16,4096]{2,1,0:T(8,128)} custom-call(f32[1,64,4096]{2,1,0:T(8,128)} %tgt_any.1, f32[2,8,4096]{2,1,0:T(8,128)} %src_any.1, f32[2]{0:T(128)} %occ.1, bf16[2,64,192]{2,1,0:T(8,128)(2,1)} %constant.6.clone.left_any, bf16[4,256,256]{2,1,0:T(8,128)(2,1)} %constant.7.clone.right_any, f32[33,64,128]{2,1,0:T(8,128)} %constant.8.clone.kern_any), custom_call_target="tpu_custom_call" | custom-call | tf_op jit(solution)/shard_map/pallas_call | solution.py:380
  44.5 1.7 %copy.8 = f32[1,16,4096]{2,1,0:T(8,128)} copy(f32[1,16,4096]{2,1,0:T(8,128)} %shard_map.64) | data formatting | bytes 524288

commit v3 on v2

--- a/solution.py
+++ b/solution.py
@@ -13,8 +13,9 @@
 MESH = pl.DeviceIdType.MESH
 LANES = 128
 CHUNKS = 4
+GATHERS = 4
 BATCH = 8
-GROUP = 16
+GROUP = 32
 
 
 def split_table(table):
@@ -77,11 +78,13 @@
 
 def body(shape, tgt_any, src_any, occ, left_any, right_any, kern_any, out,
          tgt, left, right, kern, load_sem, whole, field, part, inbox, relay, own_sem, send_sem, recv_sem, sum_send, sum_recv, relay_recv):
-    nt, ns, count, size, chunks = shape
+    nt, ns, count, size, gathers, chunks = shape
     width = size * size
     cut = width // chunks
     batch = math.gcd(BATCH, cut // LANES)
     loops = cut // LANES // batch
+    part_cut = width // gathers
+    turns = part_cut // LANES // batch
     group = math.gcd(GROUP, size)
     fold = LANES // size
     rows = part.shape[1]
@@ -103,7 +106,7 @@
 
     own = pltpu.make_async_copy(src_any, whole.at[me], own_sem)
     own.start()
-    src = whole.at[me]
+    src = src_any
     loads = [
         pltpu.make_async_copy(here_ref, there_ref, load_sem.at[i])
         for i, (here_ref, there_ref) in enumerate(
@@ -113,6 +116,9 @@
         load.start()
     pl.semaphore_wait(barrier, chips + ns - 1)
 
+    def strip(c):
+        return pl.ds(c * part_cut, part_cut)
+
     def piece(c):
         return pl.ds(c * cut, cut)
 
@@ -123,8 +129,8 @@
 
     def copy_of(c, out_slot, in_slot, origin, target, source, span):
         return pltpu.make_async_remote_copy(
-            src_ref=source.at[pl.ds(*span), :, piece(c)],
-            dst_ref=whole.at[origin, pl.ds(*span), :, piece(c)],
+            src_ref=source.at[pl.ds(*span), :, strip(c)],
+            dst_ref=whole.at[origin, pl.ds(*span), :, strip(c)],
             send_sem=send_sem.at[c, out_slot],
             recv_sem=recv_sem.at[c, in_slot],
             device_id={"tgt": target},
@@ -188,9 +194,9 @@
                 origin = beside(lax.rem(chip + step, chips))
                 arrived(c, origin, origin)
 
+    for c in range(gathers):
+        first_hop(c)
     own.wait()
-    for c in range(chunks):
-        first_hop(c)
     for load in loads[:3]:
         load.wait()
 
@@ -222,13 +228,13 @@
                     b * size:(b + 1) * size, y * count * size:(y + 1) * count * size]
         return carry
 
-    for step in range(chunks + 2):
-        if step < chunks:
+    for step in range(gathers + 2):
+        if step < gathers:
             second_hop(step)
         if step >= 2:
             complete(step - 2)
-            lax.fori_loop((step - 2) * loops, (step - 1) * loops, forward_blocks, 0)
-        if 1 <= step <= chunks:
+            lax.fori_loop((step - 2) * turns, (step - 1) * turns, forward_blocks, 0)
+        if 1 <= step <= gathers:
             third_hop(step - 1)
 
     def middle(k, carry):
@@ -372,13 +378,13 @@
     size, width = targets.shape[1], targets.shape[2]
     count, slab = sources.shape[0], sources.shape[1]
     rows = size // ns
-    chunks = CHUNKS
+    gathers, chunks = GATHERS, CHUNKS
     consts = [jnp.asarray(t) for t in tables(size, count)]
     vmem = pl.BlockSpec(memory_space=pltpu.VMEM)
     hbm = pl.BlockSpec(memory_space=pl.ANY)
     smem = pl.BlockSpec(memory_space=pltpu.SMEM)
     return pl.pallas_call(
-        functools.partial(body, (nt, ns, count, size, chunks)),
+        functools.partial(body, (nt, ns, count, size, gathers, chunks)),
         out_shape=jax.ShapeDtypeStruct((1, rows, width), jnp.float32),
         in_specs=[hbm, hbm, smem] + [hbm] * len(consts),
         out_specs=vmem,
@@ -392,8 +398,8 @@
             pltpu.VMEM((ns, rows, width), jnp.float32),
             pltpu.VMEM((rows, width), jnp.float32),
             pltpu.SemaphoreType.DMA,
-            pltpu.SemaphoreType.DMA((chunks, nt)),
-            pltpu.SemaphoreType.DMA((chunks, nt)),
+            pltpu.SemaphoreType.DMA((gathers, nt)),
+            pltpu.SemaphoreType.DMA((gathers, nt)),
             pltpu.SemaphoreType.DMA((chunks, ns)),
             pltpu.SemaphoreType.DMA((chunks, ns)),
             pltpu.SemaphoreType.DMA((chunks,)),

time: 46.3 us -> 46 us (level)
  no operation moved by 1% of the time
where the time goes in v3:
time: 46 us; the launch traced here: 45.8 us
  Pallas kernels  44.2 us (96%)
  local copies, waits for them, and re-layouts  1.67 us (4%)
    pallas_call x1, Pallas kernels, on_device(): pl.pallas_call(functools.partial(body, (nt, ns, count, size, gathers, chu...  44.2 us
    unnamed x1, local copies, waits for them, and re-layouts  1.67 us

profile of v3, /device:TPU:0, one launch (start us, length us, event | category | flops | bytes accessed | tf_op | source)
XLA Modules:
  0.0 45.8 jit_solution(12942080114852492903)
XLA Ops:
  0.0 44.2 %shard_map.64 = f32[1,16,4096]{2,1,0:T(8,128)} custom-call(f32[1,64,4096]{2,1,0:T(8,128)} %tgt_any.1, f32[2,8,4096]{2,1,0:T(8,128)} %src_any.1, f32[2]{0:T(128)} %occ.1, bf16[2,64,192]{2,1,0:T(8,128)(2,1)} %constant.6.clone.left_any, bf16[4,256,256]{2,1,0:T(8,128)(2,1)} %constant.7.clone.right_any, f32[33,64,128]{2,1,0:T(8,128)} %constant.8.clone.kern_any), custom_call_target="tpu_custom_call" | custom-call | tf_op jit(solution)/shard_map/pallas_call | solution.py:386
  44.2 1.7 %copy.8 = f32[1,16,4096]{2,1,0:T(8,128)} copy(f32[1,16,4096]{2,1,0:T(8,128)} %shard_map.64) | data formatting | bytes 524288
